TPU v7x, 32 devices: a whole 2x2x4 slice. The times are simulated.
32 devices in a mesh: grp: 4 (over y, x), ta: 8 (over z, core).
Axes of the slice: x: 2, y: 2, z: 4, core: 2. Of those that a mesh axis runs over, the one named last changes fastest.
Arguments:
- transition: float32 [256, 256], replicated, may hold values from -1 to 1, as said below
- filtered_mean: float32 [512, 256], P(('grp', 'ta')), may hold values from -6 to 6
- filtered_cov: float32 [512, 256, 256], P(('grp', 'ta')), may hold values from -1 to 2, as said below
- pred_precision: float32 [512, 256, 256], P(('grp', 'ta')), may hold values from -1 to 2, as said below
Outputs:
- smoothed_mean: float32 [512, 256], P(('grp', 'ta'))
- smoothed_cov: float32 [512, 256, 256], P(('grp', 'ta'))
Inputs may be any that keep to these rules, and one draw needn't show every extreme that they name: transition is dominated by its diagonal. Each filtered_cov at a step is symmetric with a positive diagonal. Each pred_precision at a step is symmetric with a positive diagonal.
All inputs are finite; a program needn't handle non-finite values.
Results may differ from a plain program's by a relative error of at most 0.0003.
Values sent between devices are 32-bit elements; how exact they have to be, the bound alone decides.
A program may use at most 192 MiB of HBM per device.

v0:
```python
import jax
import jax.numpy as jnp
from jax import lax
from jax.sharding import PartitionSpec as P


def carried_in(value, axis, join, neutral):
    count, mine = (lax.axis_size(axis), lax.axis_index(axis))
    pieces = jax.tree.map(lambda part: lax.all_gather(part, axis), value)
    pieces = jax.tree.map(lambda part: part[::-1], pieces)
    mine = count - 1 - mine
    subtotal = jax.tree.map(
        lambda part, zero: jnp.full_like(part, 0) + jnp.asarray(zero, part.dtype), value, neutral
    )

    def step(position, subtotal):
        longer = join(subtotal, jax.tree.map(lambda part: part[position], pieces))
        return jax.tree.map(lambda new, old: jnp.where(position < mine, new, old), longer, subtotal)

    return lax.fori_loop(0, count - 1, step, subtotal)


def spread(value, axis, source):
    kept = jnp.where(lax.axis_index(axis) == source, value, 0).astype(value.dtype)
    return lax.psum(kept, axis)


def compose(earlier, later_part):
    highest = lax.Precision.HIGHEST
    first_e, first_g, first_l = earlier
    second_e, second_g, second_l = later_part
    joined_e = jnp.matmul(first_e, second_e, precision=highest)
    joined_g = jnp.einsum("...ij,...j->...i", first_e, second_g, precision=highest) + first_g
    inner = jnp.matmul(first_e, second_l, precision=highest)
    joined_l = jnp.matmul(inner, jnp.swapaxes(first_e, -1, -2), precision=highest) + first_l
    return (joined_e, joined_g, joined_l)


def reverse_order(higher, lower):
    return compose(lower, higher)


def body(transition, filtered_mean, filtered_cov, pred_precision):
    highest = lax.Precision.HIGHEST
    steps_here = filtered_cov.shape[0]
    state_width = transition.shape[0]
    moved_cov = jnp.einsum("ij,tjk->tik", transition, filtered_cov, precision=highest)
    gain_mats = jnp.einsum("tji,tjl->til", moved_cov, pred_precision, precision=highest)
    at_end = jnp.logical_and(
        lax.axis_index("grp") == lax.axis_size("grp") - 1,
        lax.axis_index("ta") == lax.axis_size("ta") - 1,
    )
    positions = jnp.arange(steps_here, dtype=jnp.int32)
    keep_mask = jnp.where(jnp.logical_and(at_end, positions == steps_here - 1), 0.0, 1.0).astype(
        jnp.float32
    )
    gain_mats = gain_mats * keep_mask[:, None, None]
    predicted = jnp.einsum("ij,tj->ti", transition, filtered_mean, precision=highest)
    offsets = filtered_mean - jnp.einsum("tij,tj->ti", gain_mats, predicted, precision=highest)
    leftovers = filtered_cov - jnp.einsum("tij,tjk->tik", gain_mats, moved_cov, precision=highest)

    def absorb(accum, entries):
        return (compose(entries, accum), None)

    start_elem = (gain_mats[-1], offsets[-1], leftovers[-1])
    total_local, unused = lax.scan(
        absorb, start_elem, (gain_mats[:-1], offsets[:-1], leftovers[:-1]), reverse=True
    )
    identity = (
        jnp.eye(state_width, dtype=jnp.float32),
        jnp.zeros((state_width,), jnp.float32),
        jnp.zeros((state_width, state_width), jnp.float32),
    )
    after_group = carried_in(total_local, "ta", reverse_order, identity)
    group_part = compose(total_local, after_group)
    group_whole = (
        spread(group_part[0], "ta", 0),
        spread(group_part[1], "ta", 0),
        spread(group_part[2], "ta", 0),
    )
    after_groups = carried_in(group_whole, "grp", reverse_order, identity)
    carried = compose(after_group, after_groups)

    def sweep(state_pair, entries):
        mean_next, cov_next = state_pair
        gain_mat, offset, leftover = entries
        mean_out = jnp.dot(gain_mat, mean_next, precision=highest) + offset
        inner = jnp.dot(gain_mat, cov_next, precision=highest)
        cov_out = jnp.dot(inner, gain_mat.T, precision=highest) + leftover
        return ((mean_out, cov_out), (mean_out, cov_out))

    final_state, outputs = lax.scan(
        sweep, (carried[1], carried[2]), (gain_mats, offsets, leftovers), reverse=True
    )
    return (outputs[0], outputs[1])


def solution(mesh):
    return jax.shard_map(
        body,
        mesh=mesh,
        in_specs=(
            P(),
            P(("grp", "ta"), None),
            P(("grp", "ta"), None, None),
            P(("grp", "ta"), None, None),
        ),
        out_specs=(P(("grp", "ta"), None), P(("grp", "ta"), None, None)),
        check_vma=False,
    )
```

profile of v0, /device:TPU:0, one launch (start us, length us, event | category | flops | bytes accessed | tf_op | source)
XLA Modules:
  0.0 411.0 jit_solution(9666156387690830090)
XLA Ops:
  8.1 8.8 %fusion.64 = f32[16,256,256]{2,1,0:T(8,128)S(1)} fusion(f32[16,256,256]{2,1,0:T(8,128)} %param.14, f32[256,256]{1,0:T(8,128)S(1)} %copy-done), kind=kOutput, calls=%fused_computation.86 | convolution fusion | flops 3221225472 | bytes 8650752 | tf_op jit(solution)/shard_map/ij,tjk->tik/dot_general | solution.py:47
  17.0 4.5 %convolution_multiply_fusion = f32[16,256,256]{2,1,0:T(8,128)S(1)} fusion(f32[16,256,256]{2,1,0:T(8,128)S(1)} %fusion.64, f32[16,256,256]{2,1,0:T(8,128)S(1)} %copy-done.7, f32[16]{0:T(128)S(1)} %and_select_fusion), kind=kOutput, calls=%fused_computation.76 | convolution fusion | flops 3222274048 | bytes 12582976 | tf_op jit(solution)/shard_map/tji,tjl->til/dot_general | solution.py:48
  21.5 4.4 %convolution_subtract_fusion = f32[16,256,256]{2,1,0:T(8,128)S(1)} fusion(f32[16,256,256]{2,1,0:T(8,128)S(1)} %copy-done.5, f32[16,256,256]{2,1,0:T(8,128)S(1)} %convolution_multiply_fusion, f32[16,256,256]{2,1,0:T(8,128)S(1)} %fusion.64), kind=kOutput, calls=%fused_computation.75 | convolution fusion | flops 3222274048 | bytes 16777216 | tf_op jit(solution)/shard_map/tij,tjk->tik/dot_general | solution.py:60
  26.0 2.5 slice.29
  29.2 2.3 slice.27
  31.8 3.8 fusion.67
  35.6 82.2 %while.72 = (s32[]{:T(128)}, f32[256,256]{1,0:T(8,128)S(1)}, f32[256]{0:T(256)S(1)}, f32[256,256]{1,0:T(8,128)S(1)}, f32[15,256,256]{2,1,0:T(8,128)}, /*index=5*...) while((s32[]{:T(128)}, f32[256,256]{1,0:T(8,128)S(1)}, f32[256]{0:T(256)S(1)}, ...), condition=%wide.region_1.2_spmd, body=%wide.region_0.1_spmd.sunk | while | flops 604832000 | bytes 3416185 | solution.py:66
  37.0 1.4 convolution_add_fusion.7
  42.5 1.4 convolution_add_fusion.7
  47.9 1.4 convolution_add_fusion.7
  53.4 1.4 convolution_add_fusion.7
  58.9 1.4 convolution_add_fusion.7
  64.4 1.4 convolution_add_fusion.7
  69.9 1.4 convolution_add_fusion.7
  75.3 1.4 convolution_add_fusion.7
  80.8 1.4 convolution_add_fusion.7
  86.3 1.4 convolution_add_fusion.7
  119.4 13.4 %all-gather.3 = f32[8,1,256]{2,1,0:T(1,128)S(1)} all-gather(f32[1,1,256]{2,1,0:T(1,128)S(1)} %bitcast.227), channel_id=3, replica_groups=mesh['grp'=4,'ta'=8] {'ta'}, dimensions={0}, use_global_device_ids=true | all-gather | bytes 9216 | tf_op jit(solution)/shard_map/all_gather | solution.py:9
  132.9 17.7 %all-gather.14.cloned.1.call-done = f32[2048,256]{1,0:T(8,128)} async-done(((f32[256,256]{1,0:T(8,128)}), f32[2048,256]{1,0:T(8,128)}) %all-gather.14.cloned.1.call-update) | async-done | bytes 2097168 | tf_op jit(solution)/shard_map/all_gather | solution.py:9
  150.5 1.8 rev.18
  152.4 28.4 %all-gather.16.cloned.1.call-done = f32[2048,256]{1,0:T(8,128)} async-done(((f32[256,256]{1,0:T(8,128)}), f32[2048,256]{1,0:T(8,128)}) %all-gather.16.cloned.1.call-update) | async-done | bytes 2097168 | tf_op jit(solution)/shard_map/all_gather | solution.py:9
  180.8 3.0 rev.20
  183.8 18.3 %while.74 = (s32[]{:T(128)}, f32[256,256]{1,0:T(8,128)S(1)}, f32[256]{0:T(256)S(1)}, f32[256,256]{1,0:T(8,128)S(1)}, s32[]{:T(128)}, /*index=5*/f32[8,256,256]{2...) while((s32[]{:T(128)}, f32[256,256]{1,0:T(8,128)S(1)}, ...), condition=%wide.region_3.4_spmd.clone, body=%wide.region_2.3_spmd.clone.sunk | while | flops 605094912 | bytes 3943566 | solution.py:20
  202.5 2.1 fusion.62
  205.8 55.9 %all-reduce.3.cloned.1.call-done = (f32[1,256,256]{2,1,0:T(8,128)}, f32[1,256,256]{2,1,0:T(8,128)}) async-done(((f32[1,256,256]{2,1,0:T(8,128)}, f32[1,256,256]{2,1,0:T(8,128)}), (f32[1,256,256]{2,1,0:T(8,128)}, f32[1,256,256]{2,1,0:T(8,128)})) %all-reduce.3.cloned.1.call-update) | async-done | bytes 524304 | tf_op jit(solution)/shard_map/psum | solution.py:25
  262.7 13.6 %psum.22 = f32[1,256]{1,0:T(1,128)S(1)} all-reduce(f32[1,256]{1,0:T(1,128)S(1)} %bitcast.234), channel_id=1, replica_groups=mesh['grp'=4,'ta'=8] {'ta'}, use_global_device_ids=true, to_apply=%region_5.6 | all-reduce | flops 256 | bytes 2048 | tf_op jit(solution)/shard_map/psum | solution.py:25
  276.3 8.0 %all-gather.4 = f32[4,1,256]{2,1,0:T(1,128)S(1)} all-gather(f32[1,1,256]{2,1,0:T(1,128)S(1)} %bitcast.235), channel_id=1, replica_groups=mesh['grp'=4,'ta'=8] {'grp'}, dimensions={0}, use_global_device_ids=true | all-gather | bytes 5120 | tf_op jit(solution)/shard_map/all_gather | solution.py:9
  284.3 4.9 %all-gather.10.cloned.1.call-done = f32[4,256,256]{2,1,0:T(8,128)} async-done(((f32[1,256,256]{2,1,0:T(8,128)}), f32[4,256,256]{2,1,0:T(8,128)}) %all-gather.10.cloned.1.call-update) | async-done | bytes 1048592 | tf_op jit(solution)/shard_map/all_gather | solution.py:9
  290.5 27.2 %all-gather.12.cloned.1.call-done = f32[4,256,256]{2,1,0:T(8,128)} async-done(((f32[1,256,256]{2,1,0:T(8,128)}), f32[4,256,256]{2,1,0:T(8,128)}) %all-gather.12.cloned.1.call-update) | async-done | bytes 1048592 | tf_op jit(solution)/shard_map/all_gather | solution.py:9
  319.0 3.8 while.75
  323.9 2.5 broadcast_in_dim.51
  326.4 77.5 %while.73 = (s32[]{:T(128)}, f32[256]{0:T(256)S(1)}, f32[256,256]{1,0:T(8,128)S(1)}, f32[16,256]{1,0:T(8,128)S(1)}, f32[16,256,256]{2,1,0:T(8,128)}, /*index=5*/...) while((s32[]{:T(128)}, f32[256]{0:T(256)S(1)}, ...), condition=%wide.region_10.11_spmd, body=%wide.region_9.10_spmd.sunk | while | flops 403505408 | bytes 2369673 | solution.py:92
  329.1 2.2 bitcast_dynamic-update-slice_fusion.2
  333.9 2.2 bitcast_dynamic-update-slice_fusion.2
  338.8 2.2 bitcast_dynamic-update-slice_fusion.2
  343.6 2.2 bitcast_dynamic-update-slice_fusion.2
  348.5 2.2 bitcast_dynamic-update-slice_fusion.2
  353.3 2.2 bitcast_dynamic-update-slice_fusion.2
  358.1 2.2 bitcast_dynamic-update-slice_fusion.2
  363.0 2.2 bitcast_dynamic-update-slice_fusion.2
  367.8 2.2 bitcast_dynamic-update-slice_fusion.2
  372.7 2.2 bitcast_dynamic-update-slice_fusion.2
  377.5 2.2 bitcast_dynamic-update-slice_fusion.2
  382.4 2.2 bitcast_dynamic-update-slice_fusion.2
  387.2 2.2 bitcast_dynamic-update-slice_fusion.2
  392.0 2.2 bitcast_dynamic-update-slice_fusion.2
  396.9 2.2 bitcast_dynamic-update-slice_fusion.2
  401.7 2.2 bitcast_dynamic-update-slice_fusion.2
  (304 shorter events, 141.0 us)
Async XLA Ops:
  7.2 1.0 copy-start
  7.2 143.4 %all-gather.14.cloned.1.call-start = ((), (), s32[]{:S(2)}) async-start(), calls=%async_computation.2 | async-start | bytes 2359296 | tf_op jit(solution)/shard_map/all_gather | solution.py:9
  8.1 8.8 %copy-start.7 = (f32[16,256,256]{2,1,0:T(8,128)S(1)}, f32[16,256,256]{2,1,0:T(8,128)}, u32[]{:S(2)}) copy-start(f32[16,256,256]{2,1,0:T(8,128)} %param.15) | copy-start | bytes 12582916
  17.0 4.5 %copy-start.5 = (f32[16,256,256]{2,1,0:T(8,128)S(1)}, f32[16,256,256]{2,1,0:T(8,128)}, u32[]{:S(2)}) copy-start(f32[16,256,256]{2,1,0:T(8,128)} %param.14) | copy-start | bytes 12582916
  21.5 10.2 %copy-start.1 = (f32[16,256,256]{2,1,0:T(8,128)}, f32[16,256,256]{2,1,0:T(8,128)S(1)}, u32[]{:S(2)}) copy-start(f32[16,256,256]{2,1,0:T(8,128)S(1)} %convolution_multiply_fusion) | copy-start | bytes 12582916
  26.0 3.2 copy-start.4
  29.2 2.3 copy-start.8
  117.9 0.7 copy-start.2
  117.9 0.8 copy-start.6
  118.6 62.2 %all-gather.16.cloned.1.call-start = ((), (), s32[]{:S(2)}) async-start(), calls=%async_computation.3 | async-start | bytes 2359296 | tf_op jit(solution)/shard_map/all_gather | solution.py:9
  119.3 142.3 %all-reduce.3.cloned.1.call-start = ((), (), s32[]{:S(2)}) async-start(), calls=%async_computation.4 | async-start | bytes 1048576 | tf_op jit(solution)/shard_map/psum | solution.py:25
  183.8 18.3 %copy-start.3 = (f32[256,256]{1,0:T(8,128)S(1)}, f32[256,256]{1,0:T(8,128)}, u32[]{:S(2)}) copy-start(f32[256,256]{1,0:T(8,128)} %copy-done.2) | copy-start | bytes 786436
  205.7 83.5 %all-gather.10.cloned.1.call-start = ((), (), s32[]{:S(2)}) async-start(), calls=%async_computation | async-start | bytes 1310720 | tf_op jit(solution)/shard_map/all_gather | solution.py:9
  261.7 56.0 %all-gather.12.cloned.1.call-start = ((), (), s32[]{:S(2)}) async-start(), calls=%async_computation.1 | async-start | bytes 1310720 | tf_op jit(solution)/shard_map/all_gather | solution.py:9
  403.9 0.6 copy-start.9
Sparse Core Ops, SparseCore 0:
  118.7 31.7 all-gather.13
  152.1 28.5 all-gather.15
  205.8 55.8 all-reduce.2
  263.5 25.6 all-gather.9
  291.1 26.5 all-gather.11
where the time goes:
time: 415 us; the launch traced here: 411 us
  matrix products  203 us (49%)
  waiting for transfers between devices  135 us (33%)
  blocking collectives  35 us (8%)
  local copies, waits for them, and re-layouts  21.4 us (5%)
  between operations  14.1 us (3%)
    all_gather x4, waiting for transfers between devices, carried_in(): pieces = jax.tree.map(lambda part: lax.all_gather(part, axis), value)  78.2 us
    psum x1, waiting for transfers between devices, spread(): return lax.psum(kept, axis)  55.9 us
    dot_general x27, matrix products, compose(): jnp.matmul(inner, jnp.swapaxes(first_e, -1, -2), precision=highest)  35.3 us
    dot_general x16, matrix products, sweep(): cov_out = jnp.dot(inner, gain_mat.T, precision=highest) + leftover  34.5 us
    dot_general x27, matrix products, compose(): inner = jnp.matmul(first_e, second_l, precision=highest)  24.6 us
    dot_general x23, matrix products, compose(): joined_e = jnp.matmul(first_e, second_e, precision=highest)  23.8 us
    dot_general x27, matrix products, compose(): jnp.einsum('...ij,...j->...i', first_e, second_g, precision=highest)  21.7 us
    all_gather x2, blocking collectives, carried_in(): pieces = jax.tree.map(lambda part: lax.all_gather(part, axis), value)  21.4 us
  transfers between devices with their start and end apart: 5, of which 5 were waited for; matrix products, arithmetic and copies ran while one was open for 1% of the time, Pallas kernels for 0%

commit v1 on v0

--- a/solution.py
+++ b/solution.py
@@ -22,7 +22,7 @@
 
 def spread(value, axis, source):
     kept = jnp.where(lax.axis_index(axis) == source, value, 0).astype(value.dtype)
-    return lax.psum(kept, axis)
+    return jnp.sum(lax.all_gather(kept, axis), axis=0)
 
 
 def compose(earlier, later_part):

time: 415 us -> 418 us (level)
  other arithmetic: 0.38 us -> 5.32 us
    psum x1 -> x0, waiting for transfers between devices: 55.9 us -> none  [spread(): return lax.psum(kept, axis)]
    all_gather x0 -> x2, waiting for transfers between devices: none -> 55.7 us  [spread(): return jnp.sum(lax.all_gather(kept, axis), axis=0)]
    psum x1 -> x0, blocking collectives: 13.6 us -> none  [spread(): return lax.psum(kept, axis)]
    all_gather x0 -> x1, blocking collectives: none -> 10.3 us  [spread(): return jnp.sum(lax.all_gather(kept, axis), axis=0)]
    reduce_sum x0 -> x3, other arithmetic: none -> 4.94 us  [spread(): return jnp.sum(lax.all_gather(kept, axis), axis=0)]
  transfers between devices with their start and end apart: 5 -> 6, of which waited for: 5 -> 6; matrix products, arithmetic and copies ran while one was open for 1% -> 2% of each run, Pallas kernels for 0% -> 0%
where the time goes in v1:
time: 418 us; the launch traced here: 414 us
  matrix products  203 us (49%)
  waiting for transfers between devices  137 us (33%)
  blocking collectives  31.8 us (8%)
  local copies, waits for them, and re-layouts  21.4 us (5%)
  between operations  14.4 us (3%)
  other arithmetic  5.32 us (1%)
    all_gather x4, waiting for transfers between devices, carried_in(): pieces = jax.tree.map(lambda part: lax.all_gather(part, axis), value)  80.3 us
    all_gather x2, waiting for transfers between devices, spread(): return jnp.sum(lax.all_gather(kept, axis), axis=0)  55.7 us
    dot_general x27, matrix products, compose(): jnp.matmul(inner, jnp.swapaxes(first_e, -1, -2), precision=highest)  35.4 us
    dot_general x16, matrix products, sweep(): cov_out = jnp.dot(inner, gain_mat.T, precision=highest) + leftover  34.5 us
    dot_general x27, matrix products, compose(): inner = jnp.matmul(first_e, second_l, precision=highest)  24.6 us
    dot_general x23, matrix products, compose(): joined_e = jnp.matmul(first_e, second_e, precision=highest)  23.8 us
    dot_general x27, matrix products, compose(): jnp.einsum('...ij,...j->...i', first_e, second_g, precision=highest)  21.7 us
    all_gather x2, blocking collectives, carried_in(): pieces = jax.tree.map(lambda part: lax.all_gather(part, axis), value)  21.4 us
  transfers between devices with their start and end apart: 6, of which 6 were waited for; matrix products, arithmetic and copies ran while one was open for 2% of the time, Pallas kernels for 0%

profile of v1, /device:TPU:0, one launch (start us, length us, event | category | flops | bytes accessed | tf_op | source)
XLA Modules:
  0.0 414.5 jit_solution(7089845770939684419)
XLA Ops:
  8.1 8.8 %fusion.62 = f32[16,256,256]{2,1,0:T(8,128)S(1)} fusion(f32[16,256,256]{2,1,0:T(8,128)} %param.14, f32[256,256]{1,0:T(8,128)S(1)} %copy-done), kind=kOutput, calls=%fused_computation.84 | convolution fusion | flops 3221225472 | bytes 8650752 | tf_op jit(solution)/shard_map/ij,tjk->tik/dot_general | solution.py:47
  17.0 4.5 %convolution_multiply_fusion = f32[16,256,256]{2,1,0:T(8,128)S(1)} fusion(f32[16,256,256]{2,1,0:T(8,128)S(1)} %fusion.62, f32[16,256,256]{2,1,0:T(8,128)S(1)} %copy-done.7, f32[16]{0:T(128)S(1)} %and_select_fusion), kind=kOutput, calls=%fused_computation.76 | convolution fusion | flops 3222274048 | bytes 12582976 | tf_op jit(solution)/shard_map/tji,tjl->til/dot_general | solution.py:48
  21.5 4.4 %convolution_subtract_fusion = f32[16,256,256]{2,1,0:T(8,128)S(1)} fusion(f32[16,256,256]{2,1,0:T(8,128)S(1)} %copy-done.5, f32[16,256,256]{2,1,0:T(8,128)S(1)} %convolution_multiply_fusion, f32[16,256,256]{2,1,0:T(8,128)S(1)} %fusion.62), kind=kOutput, calls=%fused_computation.75 | convolution fusion | flops 3222274048 | bytes 16777216 | tf_op jit(solution)/shard_map/tij,tjk->tik/dot_general | solution.py:60
  26.0 2.5 slice.29
  29.2 2.3 slice.27
  31.8 3.8 fusion.65
  35.6 82.2 %while.72 = (s32[]{:T(128)}, f32[256,256]{1,0:T(8,128)S(1)}, f32[256]{0:T(256)S(1)}, f32[256,256]{1,0:T(8,128)S(1)}, f32[15,256,256]{2,1,0:T(8,128)}, /*index=5*...) while((s32[]{:T(128)}, f32[256,256]{1,0:T(8,128)S(1)}, f32[256]{0:T(256)S(1)}, ...), condition=%wide.region_1.2_spmd, body=%wide.region_0.1_spmd.sunk | while | flops 604832000 | bytes 3416185 | solution.py:66
  37.0 1.4 convolution_add_fusion.7
  42.4 1.4 convolution_add_fusion.7
  47.9 1.4 convolution_add_fusion.7
  58.9 1.4 convolution_add_fusion.7
  64.4 1.4 convolution_add_fusion.7
  69.9 1.4 convolution_add_fusion.7
  75.3 1.4 convolution_add_fusion.7
  119.4 13.4 %all-gather.9 = f32[8,1,256]{2,1,0:T(1,128)S(1)} all-gather(f32[1,1,256]{2,1,0:T(1,128)S(1)} %bitcast.231), channel_id=3, replica_groups=mesh['grp'=4,'ta'=8] {'ta'}, dimensions={0}, use_global_device_ids=true | all-gather | bytes 9216 | tf_op jit(solution)/shard_map/all_gather | solution.py:9
  132.9 17.6 %all-gather.19.cloned.1.call-done = f32[2048,256]{1,0:T(8,128)} async-done(((f32[256,256]{1,0:T(8,128)}), f32[2048,256]{1,0:T(8,128)}) %all-gather.19.cloned.1.call-update) | async-done | bytes 2097168 | tf_op jit(solution)/shard_map/all_gather | solution.py:9
  150.6 1.8 rev.18
  152.4 28.4 %all-gather.21.cloned.1.call-done = f32[2048,256]{1,0:T(8,128)} async-done(((f32[256,256]{1,0:T(8,128)}), f32[2048,256]{1,0:T(8,128)}) %all-gather.21.cloned.1.call-update) | async-done | bytes 2097168 | tf_op jit(solution)/shard_map/all_gather | solution.py:9
  180.8 3.0 rev.20
  183.8 18.3 %while.74 = (s32[]{:T(128)}, f32[256,256]{1,0:T(8,128)S(1)}, f32[256]{0:T(256)S(1)}, f32[256,256]{1,0:T(8,128)S(1)}, s32[]{:T(128)}, /*index=5*/f32[8,256,256]{2...) while((s32[]{:T(128)}, f32[256,256]{1,0:T(8,128)S(1)}, ...), condition=%wide.region_3.4_spmd.clone, body=%wide.region_2.3_spmd.clone.sunk | while | flops 605094912 | bytes 3943566 | solution.py:20
  202.6 2.1 fusion.61
  205.9 27.5 %all-gather.27.cloned.1.call-done = f32[2048,256]{1,0:T(8,128)} async-done(((f32[256,256]{1,0:T(8,128)}), f32[2048,256]{1,0:T(8,128)}) %all-gather.27.cloned.1.call-update) | async-done | bytes 2097168 | tf_op jit(solution)/shard_map/all_gather | solution.py:25
  233.4 2.5 reduce_sum.29
  236.0 28.1 %all-gather.23.cloned.1.call-done = f32[2048,256]{1,0:T(8,128)} async-done(((f32[256,256]{1,0:T(8,128)}), f32[2048,256]{1,0:T(8,128)}) %all-gather.23.cloned.1.call-update) | async-done | bytes 2097168 | tf_op jit(solution)/shard_map/all_gather | solution.py:25
  264.1 2.5 reduce_sum.27
  266.9 10.3 %all-gather.10 = f32[8,1,256]{2,1,0:T(1,128)S(1)} all-gather(f32[1,1,256]{2,1,0:T(1,128)S(1)} %bitcast.238), channel_id=7, replica_groups=mesh['grp'=4,'ta'=8] {'ta'}, dimensions={0}, use_global_device_ids=true | all-gather | bytes 9216 | tf_op jit(solution)/shard_map/all_gather | solution.py:25
  277.3 8.0 %all-gather.11 = f32[4,1,256]{2,1,0:T(1,128)S(1)} all-gather(f32[1,1,256]{2,1,0:T(1,128)S(1)} %bitcast.239), channel_id=8, replica_groups=mesh['grp'=4,'ta'=8] {'grp'}, dimensions={0}, use_global_device_ids=true | all-gather | bytes 5120 | tf_op jit(solution)/shard_map/all_gather | solution.py:9
  285.3 6.6 %all-gather.29.cloned.1.call-done = f32[1024,256]{1,0:T(8,128)} async-done(((f32[256,256]{1,0:T(8,128)}), f32[1024,256]{1,0:T(8,128)}) %all-gather.29.cloned.1.call-update) | async-done | bytes 1048592 | tf_op jit(solution)/shard_map/all_gather | solution.py:9
  293.2 27.6 %all-gather.25.cloned.1.call-done = f32[1024,256]{1,0:T(8,128)} async-done(((f32[256,256]{1,0:T(8,128)}), f32[1024,256]{1,0:T(8,128)}) %all-gather.25.cloned.1.call-update) | async-done | bytes 1048592 | tf_op jit(solution)/shard_map/all_gather | solution.py:9
  322.2 3.8 while.75
  327.0 2.5 broadcast_in_dim.51
  329.5 77.5 %while.73 = (s32[]{:T(128)}, f32[256]{0:T(256)S(1)}, f32[256,256]{1,0:T(8,128)S(1)}, f32[16,256]{1,0:T(8,128)S(1)}, f32[16,256,256]{2,1,0:T(8,128)}, /*index=5*/...) while((s32[]{:T(128)}, f32[256]{0:T(256)S(1)}, ...), condition=%wide.region_10.11_spmd, body=%wide.region_9.10_spmd.sunk | while | flops 403505408 | bytes 2369673 | solution.py:92
  332.2 2.2 bitcast_dynamic-update-slice_fusion.2
  337.1 2.2 bitcast_dynamic-update-slice_fusion.2
  341.9 2.2 bitcast_dynamic-update-slice_fusion.2
  346.8 2.2 bitcast_dynamic-update-slice_fusion.2
  351.6 2.2 bitcast_dynamic-update-slice_fusion.2
  356.4 2.2 bitcast_dynamic-update-slice_fusion.2
  361.3 2.2 bitcast_dynamic-update-slice_fusion.2
  366.1 2.2 bitcast_dynamic-update-slice_fusion.2
  371.0 2.2 bitcast_dynamic-update-slice_fusion.2
  375.8 2.2 bitcast_dynamic-update-slice_fusion.2
  380.6 2.2 bitcast_dynamic-update-slice_fusion.2
  385.5 2.2 bitcast_dynamic-update-slice_fusion.2
  390.3 2.2 bitcast_dynamic-update-slice_fusion.2
  395.2 2.2 bitcast_dynamic-update-slice_fusion.2
  400.0 2.2 bitcast_dynamic-update-slice_fusion.2
  404.9 2.2 bitcast_dynamic-update-slice_fusion.2
  (310 shorter events, 144.9 us)
Async XLA Ops:
  7.2 1.0 copy-start
  7.2 143.4 %all-gather.19.cloned.1.call-start = ((), (), s32[]{:S(2)}) async-start(), calls=%async_computation | async-start | bytes 2359296 | tf_op jit(solution)/shard_map/all_gather | solution.py:9
  8.1 8.8 %copy-start.7 = (f32[16,256,256]{2,1,0:T(8,128)S(1)}, f32[16,256,256]{2,1,0:T(8,128)}, u32[]{:S(2)}) copy-start(f32[16,256,256]{2,1,0:T(8,128)} %param.15) | copy-start | bytes 12582916
  17.0 4.5 %copy-start.5 = (f32[16,256,256]{2,1,0:T(8,128)S(1)}, f32[16,256,256]{2,1,0:T(8,128)}, u32[]{:S(2)}) copy-start(f32[16,256,256]{2,1,0:T(8,128)} %param.14) | copy-start | bytes 12582916
  21.5 10.2 %copy-start.1 = (f32[16,256,256]{2,1,0:T(8,128)}, f32[16,256,256]{2,1,0:T(8,128)S(1)}, u32[]{:S(2)}) copy-start(f32[16,256,256]{2,1,0:T(8,128)S(1)} %convolution_multiply_fusion) | copy-start | bytes 12582916
  26.0 3.2 copy-start.4
  29.2 2.3 copy-start.8
  117.8 0.7 copy-start.2
  117.9 0.8 copy-start.6
  118.6 62.2 %all-gather.21.cloned.1.call-start = ((), (), s32[]{:S(2)}) async-start(), calls=%async_computation.1 | async-start | bytes 2359296 | tf_op jit(solution)/shard_map/all_gather | solution.py:9
  119.4 114.1 %all-gather.27.cloned.1.call-start = ((), (), s32[]{:S(2)}) async-start(), calls=%async_computation.4 | async-start | bytes 2359296 | tf_op jit(solution)/shard_map/all_gather | solution.py:25
  183.8 18.3 %copy-start.3 = (f32[256,256]{1,0:T(8,128)S(1)}, f32[256,256]{1,0:T(8,128)}, u32[]{:S(2)}) copy-start(f32[256,256]{1,0:T(8,128)} %copy-done.2) | copy-start | bytes 786436
  204.7 59.4 %all-gather.23.cloned.1.call-start = ((), (), s32[]{:S(2)}) async-start(), calls=%async_computation.2 | async-start | bytes 2359296 | tf_op jit(solution)/shard_map/all_gather | solution.py:25
  205.8 86.1 %all-gather.29.cloned.1.call-start = ((), (), s32[]{:S(2)}) async-start(), calls=%async_computation.5 | async-start | bytes 1310720 | tf_op jit(solution)/shard_map/all_gather | solution.py:9
  235.9 85.0 %all-gather.25.cloned.1.call-start = ((), (), s32[]{:S(2)}) async-start(), calls=%async_computation.3 | async-start | bytes 1310720 | tf_op jit(solution)/shard_map/all_gather | solution.py:9
  407.0 0.6 copy-start.9
Sparse Core Ops, SparseCore 0:
  118.7 31.7 all-gather.18
  152.2 28.5 all-gather.20
  204.8 28.5 all-gather.26
  235.4 28.5 all-gather.22
  265.8 26.1 all-gather.28
  294.2 26.6 all-gather.24
